TPU v7x, 512 devices: a whole 4x8x8 slice. The times are simulated.
512 devices in a mesh: dp: 256 (over x, z, y), cent: 2 (over core).
Axes of the slice: x: 4, y: 8, z: 8, core: 2. Of those that a mesh axis runs over, the one named last changes fastest.
Arguments:
- tokens: float32 [30720, 128], P('dp'), may hold values from -6 to 6
- centroids: float32 [32768, 128], P(('dp', 'cent')), may hold values from -6 to 6
Outputs:
- new_centroids: float32 [32768, 128], P(('dp', 'cent'))
- residuals: float32 [30720, 128], P('dp')
All inputs are finite; a program needn't handle non-finite values.
Results may differ from a plain program's by a relative error of at most 0.0005.
The roundings to bfloat16 on the way count: a program that leaves them out, or rounds other values in their place, can miss the bound.
Values may be sent and summed in bfloat16 or wider, within the bound.
A program may use at most 64 MiB of HBM per device.

v0:
```python
import jax
import jax.numpy as jnp
from jax import lax
from jax.sharding import PartitionSpec as P

ITERS = 3
KB = 2048
EPSILON = 1e-06
SOFTMAX_WARMTH = 0.05


def normalized_rows(values):
    return values * lax.rsqrt(jnp.mean(values * values, axis=-1, keepdims=True) + EPSILON)


def exponent_block(token_half_rows, block):
    affinity_scores = lax.dot_general(
        token_half_rows, block, (((1,), (1,)), ((), ())), preferred_element_type=jnp.float32
    )
    return jnp.exp((affinity_scores / token_half_rows.shape[1] - 1.0) / SOFTMAX_WARMTH)


def shards(tokens, centroids):
    rows_here, feature_dim = tokens.shape
    unit_tok = normalized_rows(tokens)
    token_half_rows = unit_tok.astype(jnp.bfloat16)
    own_rows = normalized_rows(centroids).astype(jnp.bfloat16)
    columns = lax.all_gather(own_rows, "dp", axis=0, tiled=True)
    col_count = columns.shape[0]
    block_count = col_count // KB
    blocks = columns.reshape(block_count, KB, feature_dim)
    col_mass = rows_here * lax.axis_size("dp") / (col_count * lax.axis_size("cent"))
    scales = jnp.ones((block_count, KB), jnp.float32)
    assignment_weight = jnp.ones((rows_here,), jnp.float32)
    for step_index in range(ITERS):

        def row_step(total, packed):
            kernel = exponent_block(token_half_rows, packed[0])
            return (total + jnp.sum(kernel * packed[1][None, :], axis=1), None)

        row_half = lax.scan(row_step, jnp.zeros((rows_here,), jnp.float32), (blocks, scales))[0]
        row_sum = lax.psum(row_half, "cent")
        assignment_weight = 1.0 / row_sum

        def col_only(block):
            kernel = exponent_block(token_half_rows, block)
            return jnp.sum(kernel * assignment_weight[:, None], axis=0)

        col_flat = lax.map(col_only, blocks).reshape(col_count)
        col_total = lax.psum(col_flat, "dp")
        scales = (col_mass / col_total).reshape(block_count, KB)
    weights_bf = assignment_weight.astype(jnp.bfloat16)
    pieces = (
        lax.all_gather(token_half_rows, "dp", axis=0, tiled=True),
        lax.all_gather(weights_bf, "dp", axis=0, tiled=True),
    )
    kernel = exponent_block(pieces[0], own_rows)
    assign_bf = (kernel * pieces[1].astype(jnp.float32)[:, None]).astype(jnp.bfloat16)
    sums_own = lax.dot_general(
        assign_bf, pieces[0], (((0,), (0,)), ((), ())), preferred_element_type=jnp.float32
    )
    new_own = normalized_rows(sums_own)
    fresh = lax.all_gather(new_own.astype(jnp.bfloat16), "dp", axis=0, tiled=True)
    fresh_blocks = fresh.reshape(block_count, KB, feature_dim)

    def soft_step(total, packed):
        kernel = exponent_block(token_half_rows, packed[0])
        transport_plan_half = (kernel * assignment_weight[:, None] * packed[1][None, :]).astype(
            jnp.bfloat16
        )
        return (
            total + jnp.dot(transport_plan_half, packed[2], preferred_element_type=jnp.float32),
            None,
        )

    soft_half = lax.scan(
        soft_step, jnp.zeros((rows_here, feature_dim), jnp.float32), (blocks, scales, fresh_blocks)
    )[0]
    soft = lax.psum(soft_half, "cent")
    return (new_own, unit_tok - soft)


def solution(mesh):
    in_specs = (P("dp", None), P(("dp", "cent"), None))
    out_specs = (P(("dp", "cent"), None), P("dp", None))
    return jax.shard_map(shards, mesh=mesh, in_specs=in_specs, out_specs=out_specs, check_vma=False)
```

profile of v0, /device:TPU:1, one launch (start us, length us, event | category | flops | bytes accessed | tf_op | source)
XLA Modules:
  0.0 2422.9 jit_solution(2898249756367351308)
XLA Ops:
  11.5 130.1 %all-gather.6.cloned.1.call-done = bf16[16384,128]{1,0:T(8,128)(2,1)} async-done(((bf16[64,128]{1,0:T(8,128)(2,1)}), bf16[16384,128]{1,0:T(8,128)(2,1)}) %all-gather.6.cloned.1.call-update) | async-done | bytes 4194320 | tf_op jit(solution)/shard_map/all_gather | solution.py:28
  141.6 13.4 while.91
  155.1 6.3 psum.49
  161.3 14.4 while.88
  176.4 218.9 %all-reduce.5.cloned.1.call-done = f32[16384]{0:T(1024)} async-done(((f32[16384]{0:T(1024)}), f32[16384]{0:T(1024)}) %all-reduce.5.cloned.1.call-update) | async-done | bytes 65552 | tf_op jit(solution)/shard_map/psum | solution.py:50
  396.2 13.7 while.92
  409.9 7.2 psum.51
  417.1 14.4 while.89
  434.8 214.8 %all-reduce.7.cloned.1.call-done = f32[16384]{0:T(1024)} async-done(((f32[16384]{0:T(1024)}), f32[16384]{0:T(1024)}) %all-reduce.7.cloned.1.call-update) | async-done | bytes 65552 | tf_op jit(solution)/shard_map/psum | solution.py:50
  650.4 13.7 while.93
  664.1 7.2 psum.53
  671.6 1146.0 %all-reduce = bf16[30720]{0:T(1024)(128)(2,1)S(1)} all-reduce(bf16[30720]{0:T(1024)(128)(2,1)S(1)} %dynamic-update-slice), channel_id=1, replica_groups=mesh['dp'=256,'cent'=2] {'dp'}, use_global_device_ids=true, to_apply=%add | all-reduce | flops 30720 | bytes 122880
  1817.6 14.4 while.90
  1832.7 9.6 multiply_reduce_fusion.1
  1843.0 421.1 %all-reduce.9.cloned.1.call-done = f32[16384]{0:T(1024)} async-done(((f32[16384]{0:T(1024)}), f32[16384]{0:T(1024)}) %all-reduce.9.cloned.1.call-update) | async-done | bytes 65552 | tf_op jit(solution)/shard_map/psum | solution.py:50
  2265.0 126.2 %all-gather.8.cloned.1.call-done = bf16[16384,128]{1,0:T(8,128)(2,1)} async-done(((bf16[64,128]{1,0:T(8,128)(2,1)}), bf16[16384,128]{1,0:T(8,128)(2,1)}) %all-gather.8.cloned.1.call-update) | async-done | bytes 4194320 | tf_op jit(solution)/shard_map/all_gather | solution.py:63
  2391.2 16.6 while.94
  2391.2 2.0 fusion.144
  2393.3 2.0 fusion.144
  2395.4 2.0 fusion.144
  2397.4 2.0 fusion.144
  2399.5 2.0 fusion.144
  2401.6 2.0 fusion.144
  2407.8 7.5 psum.55
  (175 shorter events, 99.2 us)
Async XLA Ops:
  7.2 134.5 %all-gather.6.cloned.1.call-start = ((), (), s32[]{:S(2)}) async-start(), calls=%async_computation.1 | async-start | bytes 4210688 | tf_op jit(solution)/shard_map/all_gather | solution.py:28
  9.6 385.8 %all-reduce.5.cloned.1.call-start = ((), (), s32[]{:S(2)}) async-start(), calls=%async_computation.2 | async-start | bytes 131072 | tf_op jit(solution)/shard_map/psum | solution.py:50
  176.4 473.2 %all-reduce.7.cloned.1.call-start = ((), (), s32[]{:S(2)}) async-start(), calls=%async_computation.3 | async-start | bytes 131072 | tf_op jit(solution)/shard_map/psum | solution.py:50
  431.5 0.7 copy-start.1
  432.2 1400.5 %all-gather.4.cloned.1.call-start = ((), (), s32[]{:S(2)}) async-start(), calls=%async_computation | async-start | bytes 7895040 | tf_op jit(solution)/shard_map/all_gather | solution.py:54
  432.7 1831.4 %all-reduce.9.cloned.1.call-start = ((), (), s32[]{:S(2)}) async-start(), calls=%async_computation.4 | async-start | bytes 131072 | tf_op jit(solution)/shard_map/psum | solution.py:50
  1817.6 15.1 copy-start.3
  1832.6 558.6 %copy-start.2 = (bf16[120,128]{1,0:T(8,128)(2,1)S(1)}, bf16[120,128]{1,0:T(8,128)(2,1)}, u32[]{:S(2)}) copy-start(bf16[120,128]{1,0:T(8,128)(2,1)} %get-tuple-element.1021) | copy-start | bytes 92164
  1832.6 558.6 %all-gather.8.cloned.1.call-start = ((), (), s32[]{:S(2)}) async-start(), calls=%async_computation.5 | async-start | bytes 4210688 | tf_op jit(solution)/shard_map/all_gather | solution.py:63
  2391.2 24.1 copy-start
Sparse Core Ops, SparseCore 0:
  12.9 128.6 all-gather.5
  176.5 218.8 all-reduce.4
  432.3 217.2 all-reduce.6
  654.4 129.2 all-gather.3
  1832.7 431.3 all-reduce.8
  2269.1 122.0 all-gather.7
where the time goes:
time: 2430 us; the launch traced here: 2420 us
  blocking collectives  1170 us (48%)
  waiting for transfers between devices  1110 us (46%)
  matrix products  103 us (4%)
    unnamed x1, blocking collectives  1150 us
    psum x3, waiting for transfers between devices, shards(): col_total = lax.psum(col_flat, 'dp')  855 us
    all_gather x1, waiting for transfers between devices, shards(): columns = lax.all_gather(own_rows, 'dp', axis=0, tiled=True)  130 us
    all_gather x1, waiting for transfers between devices, shards(): lax.all_gather(new_own.astype(jnp.bfloat16), 'dp', axis=0, tiled=True)  126 us
    dot_general x48, matrix products, exponent_block(): lax.dot_general(token_half_rows, block, (((1,), (1,)), ((), ())), preferr...  77.1 us
  transfers between devices with their start and end apart: 6, of which 5 were waited for; matrix products, arithmetic and copies ran while one was open for 2% of the time, Pallas kernels for 0%

commit v1 on v0

--- a/solution.py
+++ b/solution.py
@@ -47,7 +47,7 @@
             return jnp.sum(kernel * assignment_weight[:, None], axis=0)
 
         col_flat = lax.map(col_only, blocks).reshape(col_count)
-        col_total = lax.psum(col_flat, "dp")
+        col_total = jnp.sum(lax.all_gather(col_flat, "dp"), axis=0)
         scales = (col_mass / col_total).reshape(block_count, KB)
     weights_bf = assignment_weight.astype(jnp.bfloat16)
     pieces = (

time: 2430 us -> 2100 us (0.86)
  waiting for transfers between devices: 1110 us -> 759 us
  other arithmetic: 8.49 us -> 42.3 us
    psum x3 -> x0, waiting for transfers between devices: 855 us -> none  [shards(): col_total = lax.psum(col_flat, 'dp')]
    all_gather x0 -> x3, waiting for transfers between devices: none -> 310 us  [shards(): col_total = jnp.sum(lax.all_gather(col_flat, 'dp'), axis=0)]
    all_gather x1, waiting for transfers between devices: 126 us -> 318 us  [shards(): lax.all_gather(new_own.astype(jnp.bfloat16), 'dp', axis=0, tiled=True)]
    reduce_sum x0 -> x3, other arithmetic: none -> 36.3 us  [shards(): col_total = jnp.sum(lax.all_gather(col_flat, 'dp'), axis=0)]
  transfers between devices with their start and end apart: 6 -> 6, of which waited for: 5 -> 4; matrix products, arithmetic and copies ran while one was open for 2% -> 3% of each run, Pallas kernels for 0% -> 0%
where the time goes in v1:
time: 2100 us
  blocking collectives  1170 us (56%)
  waiting for transfers between devices  759 us (36%)
  matrix products  102 us (5%)
  other arithmetic  42.3 us (2%)
    unnamed x1, blocking collectives  1150 us
    all_gather x1, waiting for transfers between devices, shards(): lax.all_gather(new_own.astype(jnp.bfloat16), 'dp', axis=0, tiled=True)  318 us
    all_gather x3, waiting for transfers between devices, shards(): col_total = jnp.sum(lax.all_gather(col_flat, 'dp'), axis=0)  310 us
    all_gather x1, waiting for transfers between devices, shards(): columns = lax.all_gather(own_rows, 'dp', axis=0, tiled=True)  130 us
    dot_general x48, matrix products, exponent_block(): lax.dot_general(token_half_rows, block, (((1,), (1,)), ((), ())), preferr...  77.2 us
  transfers between devices with their start and end apart: 6, of which 4 were waited for; matrix products, arithmetic and copies ran while one was open for 3% of the time, Pallas kernels for 0%

profile of v1, /device:TPU:1, one launch (start us, length us, event | category | flops | bytes accessed | tf_op | source)
XLA Modules:
  0.0 2097.4 jit_solution(9791629101928616582)
XLA Ops:
  11.5 130.1 %all-gather.12.cloned.1.call-done = bf16[16384,128]{1,0:T(8,128)(2,1)} async-done(((bf16[64,128]{1,0:T(8,128)(2,1)}), bf16[16384,128]{1,0:T(8,128)(2,1)}) %all-gather.12.cloned.1.call-update) | async-done | bytes 4194320 | tf_op jit(solution)/shard_map/all_gather | solution.py:28
  141.6 13.4 while.91
  155.1 6.3 psum.28
  161.3 14.4 while.88
  176.5 154.9 %all-gather.16.cloned.1.call-done = f32[256,1,16384]{2,1,0:T(1,128)} async-done(((f32[1,1,16384]{2,1,0:T(1,128)}), f32[256,1,16384]{2,1,0:T(1,128)}) %all-gather.16.cloned.1.call-update) | async-done | bytes 16777232 | tf_op jit(solution)/shard_map/all_gather | solution.py:50
  331.4 12.1 reduce_sum.128
  343.6 13.7 while.92
  357.3 3.3 psum.29
  360.6 14.4 while.89
  376.4 154.7 %all-gather.18.cloned.1.call-done = f32[256,1,16384]{2,1,0:T(1,128)} async-done(((f32[1,1,16384]{2,1,0:T(1,128)}), f32[256,1,16384]{2,1,0:T(1,128)}) %all-gather.18.cloned.1.call-update) | async-done | bytes 16777232 | tf_op jit(solution)/shard_map/all_gather | solution.py:50
  531.1 12.1 reduce_sum.129
  543.3 13.7 while.93
  557.0 3.3 psum.30
  560.4 14.4 while.90
  577.7 1148.6 %all-reduce = bf16[30720]{0:T(1024)(128)(2,1)S(1)} all-reduce(bf16[30720]{0:T(1024)(128)(2,1)S(1)} %dynamic-update-slice), channel_id=1, replica_groups=mesh['dp'=256,'cent'=2] {'dp'}, use_global_device_ids=true, to_apply=%add | all-reduce | flops 30720 | bytes 122880
  1726.3 9.6 multiply_reduce_fusion.1
  1736.7 12.1 reduce_sum.131
  1748.8 318.3 %all-gather.14.cloned.1.call-done = bf16[16384,128]{1,0:T(8,128)(2,1)} async-done(((bf16[64,128]{1,0:T(8,128)(2,1)}), bf16[16384,128]{1,0:T(8,128)(2,1)}) %all-gather.14.cloned.1.call-update) | async-done | bytes 4194320 | tf_op jit(solution)/shard_map/all_gather | solution.py:63
  2067.1 15.2 while.94
  2067.1 1.9 fusion.144
  2072.8 1.9 fusion.144
  2076.6 1.9 fusion.144
  2080.4 1.9 fusion.144
  2082.3 7.5 psum.31
  (178 shorter events, 100.3 us)
Async XLA Ops:
  7.2 134.5 %all-gather.12.cloned.1.call-start = ((), (), s32[]{:S(2)}) async-start(), calls=%async_computation.1 | async-start | bytes 4210688 | tf_op jit(solution)/shard_map/all_gather | solution.py:28
  9.6 321.9 %all-gather.16.cloned.1.call-start = ((), (), s32[]{:S(2)}) async-start(), calls=%async_computation.3 | async-start | bytes 16842752 | tf_op jit(solution)/shard_map/all_gather | solution.py:50
  176.4 354.7 %all-gather.18.cloned.1.call-start = ((), (), s32[]{:S(2)}) async-start(), calls=%async_computation.4 | async-start | bytes 16842752 | tf_op jit(solution)/shard_map/all_gather | solution.py:50
  375.0 0.8 copy-start.1
  375.7 1350.6 %all-gather.10.cloned.1.call-start = ((), (), s32[]{:S(2)}) async-start(), calls=%async_computation | async-start | bytes 7895040 | tf_op jit(solution)/shard_map/all_gather | solution.py:54
  376.3 1360.4 %all-gather.20.cloned.1.call-start = ((), (), s32[]{:S(2)}) async-start(), calls=%async_computation.5 | async-start | bytes 16842752 | tf_op jit(solution)/shard_map/all_gather | solution.py:50
  376.4 166.9 %copy-start.2 = (bf16[120,128]{1,0:T(8,128)(2,1)S(1)}, bf16[120,128]{1,0:T(8,128)(2,1)}, u32[]{:S(2)}) copy-start(bf16[120,128]{1,0:T(8,128)(2,1)} %copy-done.1) | copy-start | bytes 92164
  560.4 1166.0 %copy-start.3 = (bf16[64,128]{1,0:T(8,128)(2,1)S(1)}, bf16[64,128]{1,0:T(8,128)(2,1)}, u32[]{:S(2)}) copy-start(bf16[64,128]{1,0:T(8,128)(2,1)} %multiply_convert_fusion.1) | copy-start | bytes 49156
  575.5 1491.6 %all-gather.14.cloned.1.call-start = ((), (), s32[]{:S(2)}) async-start(), calls=%async_computation.2 | async-start | bytes 4210688 | tf_op jit(solution)/shard_map/all_gather | solution.py:63
  2067.1 22.7 %copy-start = (f32[120,128]{1,0:T(8,128)S(1)}, f32[120,128]{1,0:T(8,128)}, u32[]{:S(2)}) copy-start(f32[120,128]{1,0:T(8,128)} %param.16) | copy-start | bytes 184324
Sparse Core Ops, SparseCore 0:
  12.9 128.6 all-gather.11
  176.6 154.8 all-gather.15
  375.9 155.2 all-gather.17
  536.0 127.7 all-gather.9
  668.1 157.4 all-gather.19
  1736.8 330.2 all-gather.13
